TPU v7x, 32 devices: a whole 2x2x4 slice. The times are simulated.
32 devices in a mesh: gz: 4 (over y, core), wa: 8 (over z, x).
Axes of the slice: x: 2, y: 2, z: 4, core: 2. Of those that a mesh axis runs over, the one named last changes fastest.
Arguments:
- positions: float32 [3, 32768], P(None, ('gz', 'wa')), may hold values from -1.5 to 1.5
- forces: float32 [3, 32768], P(None, ('gz', 'wa')), may hold values from -6 to 6
- order: int32 [32768], P(('gz', 'wa')), may hold values from 0 to 1023, as said below
- pair_list: int32 [1792, 2], P('gz'), may hold values from 0 to 63, as said below
- pair_worker: int32 [1792], P('gz'), may hold values from 0 to 8, as said below
Outputs:
- velocities: float32 [3, 32768], P(None, ('gz', 'wa'))
Inputs may be any that keep to these rules, and one draw needn't show every extreme that they name: `order`: each device's 1024 entries are a permutation of 0 to 1023. `pair_list`: in each layer's 448 rows column 0 is a block of that layer (index within the layer) and column 1 a block of that layer, or 32 plus the index of a block of the layer above; no unordered pair of blocks is listed twice in a layer; every block of a layer is paired with itself once. `pair_worker`: within one layer no worker is named by more than 56 rows, and in some layer every worker is named by exactly 56; rows of the top layer whose column 1 is 32 or more are marked 8.
All inputs are finite; a program needn't handle non-finite values.
Results may differ from a plain program's by a relative error of at most 0.00014.
Values sent between devices are 32-bit elements; how exact they have to be, the bound alone decides.
A program may use at most 64 MiB of HBM per device.

v0:
```python
import math

import jax
import jax.numpy as jnp
from jax import lax
from jax.sharding import PartitionSpec as P

BS = 256


radius = 0.25
screening = 1.0
prefactor = 1.0 / (4.0 * math.pi)


def passed_along(value, axis, by):
    length = lax.axis_size(axis)
    pairs = [(i, i + by) for i in range(length) if 0 <= i + by < length]
    return lax.ppermute(value, axis, pairs)


def tile_terms(coords_a, loads_a, coords_b, loads_b):
    highest = lax.Precision.HIGHEST
    offset = coords_a[:, :, :, None] - coords_b[:, :, None, :]
    squared = jnp.sum(offset * offset, axis=1) + radius * radius
    distance = jnp.sqrt(squared)
    screen = jax.scipy.special.erfc(screening * distance)
    gaussian = screening / math.sqrt(math.pi) * jnp.exp(-screening * screening * squared)
    isotropic = screen / distance * (0.75 + 0.5 * radius * radius / squared) + 0.5 * gaussian
    dyadic = (
        screen / (distance * squared) * (0.75 - 1.5 * radius * radius / squared)
        + 0.5 * gaussian / squared
    )
    project_b = jnp.einsum("kcij,kcj->kij", offset, loads_b, precision=highest)
    project_a = jnp.einsum("kcij,kci->kij", offset, loads_a, precision=highest)
    result_a = jnp.einsum("kij,kcj->kci", isotropic, loads_b, precision=highest) + jnp.einsum(
        "kcij,kij->kci", offset, dyadic * project_b, precision=highest
    )
    result_b = jnp.einsum("kij,kci->kcj", isotropic, loads_a, precision=highest) + jnp.einsum(
        "kcij,kij->kcj", offset, dyadic * project_a, precision=highest
    )
    return (prefactor * result_a, prefactor * result_b)


def body(positions, forces, order, pair_list, pair_worker):
    per_dev = positions.shape[1]
    nblocks = per_dev // BS
    coords = positions[:, order].reshape(3, nblocks, BS).transpose(1, 0, 2)
    loads = forces[:, order].reshape(3, nblocks, BS).transpose(1, 0, 2)
    payload = jnp.concatenate([coords, loads], axis=1)
    slab = lax.all_gather(payload, "wa", axis=0, tiled=True)
    upper = passed_along(slab, "gz", -1)
    layer = slab.shape[0]
    blocks = jnp.concatenate([slab, upper], axis=0)
    capacity = 14 * nblocks
    worker = lax.axis_index("wa")
    mine = pair_worker == worker
    rank = jnp.cumsum(mine.astype(jnp.int32)) - 1
    target = jnp.where(mine, rank, capacity)
    chosen = (
        jnp.zeros((capacity,), jnp.int32)
        .at[target]
        .set(jnp.arange(pair_worker.shape[0], dtype=jnp.int32), mode="drop")
    )
    filled = jnp.sum(mine.astype(jnp.int32))
    active = (jnp.arange(capacity, dtype=jnp.int32) < filled).astype(jnp.float32)
    first = pair_list[chosen, 0]
    second = pair_list[chosen, 1]
    twice = active * (first != second).astype(jnp.float32)
    items = (
        first.reshape(14, nblocks),
        second.reshape(14, nblocks),
        active.reshape(14, nblocks),
        twice.reshape(14, nblocks),
    )

    def step(total, item):
        first_ids, second_ids, weight_a, weight_b = item
        block_a = blocks[first_ids]
        block_b = blocks[second_ids]
        result_a, result_b = tile_terms(
            block_a[:, :3], block_a[:, 3:], block_b[:, :3], block_b[:, 3:]
        )
        total = total.at[first_ids].add(weight_a[:, None, None] * result_a)
        total = total.at[second_ids].add(weight_b[:, None, None] * result_b)
        return (total, None)

    partial_value, _ = lax.scan(step, jnp.zeros((2 * layer, 3, BS), jnp.float32), items)
    lower_part = partial_value[:layer]
    upper_part = partial_value[layer:]
    returned = passed_along(upper_part, "gz", 1)
    owned = lax.psum_scatter(lower_part + returned, "wa", scatter_dimension=0, tiled=True)
    blocked = owned.transpose(1, 0, 2).reshape(3, per_dev)
    return jnp.zeros((3, per_dev), jnp.float32).at[:, order].set(blocked)


def solution(mesh):
    return jax.shard_map(
        body,
        mesh=mesh,
        in_specs=(
            P(None, ("gz", "wa")),
            P(None, ("gz", "wa")),
            P(("gz", "wa")),
            P("gz", None),
            P("gz"),
        ),
        out_specs=P(None, ("gz", "wa")),
        check_vma=False,
    )
```

profile of v0, /device:TPU:0, one launch (start us, length us, event | category | flops | bytes accessed | tf_op | source)
XLA Modules:
  0.0 613.0 jit_solution(1797622766810007707)
XLA Ops:
  15.2 32.5 %all_gather.3 = f32[32,6,256]{2,1,0:T(8,128)S(1)} all-gather(f32[4,6,256]{2,1,0:T(8,128)S(1)} %pad_maximum_fusion.1), channel_id=1, replica_groups=mesh['gz'=4,'wa'=8] {'wa'}, dimensions={0}, use_global_device_ids=true | all-gather | bytes 221184 | tf_op jit(solution)/shard_map/all_gather | solution.py:51
  57.9 464.8 %while.12 = (s32[]{:T(128)}, f32[64,3,256]{2,1,0:T(4,128)S(1)}, s32[14,4]{1,0:T(8,128)S(1)}, s32[14,4]{1,0:T(8,128)S(1)}, f32[64,6,256]{2,1,0:T(8,128)S(1)}, /*i...) while((s32[]{:T(128)}, f32[64,3,256]{2,1,0:T(4,128)S(1)}, s32[14,4]{1,0:T(8,128)S(1)}, ...), condition=%wide.region_8.9_spmd, body=%wide.region_4.8_spmd.sunk | while | flops 65291296 | bytes 41436504 | solution.py:88
  61.8 11.7 %fusion.86 = f32[4,256,1,256]{3,2,1,0:T(1,128)S(1)} fusion(f32[4,3,256,1]{1,3,2,0:T(1,128)S(1)} %copy.67, f32[4,3,256,256]{3,2,1,0:T(8,128)} %get-tuple-element.189), kind=kOutput, calls=%fused_computation.10.clone.1 | convolution fusion | flops 9437184 | bytes 4206592 | tf_op jit(solution)/shard_map/while/body/eval_jaxpr/kcij,kci->kij/dot_general | solution.py:35
  95.0 11.7 %fusion.86 = f32[4,256,1,256]{3,2,1,0:T(1,128)S(1)} fusion(f32[4,3,256,1]{1,3,2,0:T(1,128)S(1)} %copy.67, f32[4,3,256,256]{3,2,1,0:T(8,128)} %get-tuple-element.189), kind=kOutput, calls=%fused_computation.10.clone.1 | convolution fusion | flops 9437184 | bytes 4206592 | tf_op jit(solution)/shard_map/while/body/eval_jaxpr/kcij,kci->kij/dot_general | solution.py:35
  112.1 9.7 %fusion.91 = f32[4,256,1,3]{3,2,1,0:T(1,128)S(1)} fusion(f32[4,3,256,256]{3,2,1,0:T(8,128)S(1)} %copy-done.1, f32[4,256,256,1]{2,1,0,3:T(8,128)S(1)} %fusion.90), kind=kOutput, calls=%fused_computation.12.clone.1 | convolution fusion | flops 9437184 | bytes 4206592 | tf_op jit(solution)/shard_map/while/body/eval_jaxpr/kcij,kij->kci/dot_general | solution.py:36
  128.2 11.7 %fusion.86 = f32[4,256,1,256]{3,2,1,0:T(1,128)S(1)} fusion(f32[4,3,256,1]{1,3,2,0:T(1,128)S(1)} %copy.67, f32[4,3,256,256]{3,2,1,0:T(8,128)} %get-tuple-element.189), kind=kOutput, calls=%fused_computation.10.clone.1 | convolution fusion | flops 9437184 | bytes 4206592 | tf_op jit(solution)/shard_map/while/body/eval_jaxpr/kcij,kci->kij/dot_general | solution.py:35
  161.3 11.7 %fusion.86 = f32[4,256,1,256]{3,2,1,0:T(1,128)S(1)} fusion(f32[4,3,256,1]{1,3,2,0:T(1,128)S(1)} %copy.67, f32[4,3,256,256]{3,2,1,0:T(8,128)} %get-tuple-element.189), kind=kOutput, calls=%fused_computation.10.clone.1 | convolution fusion | flops 9437184 | bytes 4206592 | tf_op jit(solution)/shard_map/while/body/eval_jaxpr/kcij,kci->kij/dot_general | solution.py:35
  178.5 9.7 %fusion.91 = f32[4,256,1,3]{3,2,1,0:T(1,128)S(1)} fusion(f32[4,3,256,256]{3,2,1,0:T(8,128)S(1)} %copy-done.1, f32[4,256,256,1]{2,1,0,3:T(8,128)S(1)} %fusion.90), kind=kOutput, calls=%fused_computation.12.clone.1 | convolution fusion | flops 9437184 | bytes 4206592 | tf_op jit(solution)/shard_map/while/body/eval_jaxpr/kcij,kij->kci/dot_general | solution.py:36
  194.5 11.6 %fusion.86 = f32[4,256,1,256]{3,2,1,0:T(1,128)S(1)} fusion(f32[4,3,256,1]{1,3,2,0:T(1,128)S(1)} %copy.67, f32[4,3,256,256]{3,2,1,0:T(8,128)} %get-tuple-element.189), kind=kOutput, calls=%fused_computation.10.clone.1 | convolution fusion | flops 9437184 | bytes 4206592 | tf_op jit(solution)/shard_map/while/body/eval_jaxpr/kcij,kci->kij/dot_general | solution.py:35
  227.7 11.7 %fusion.86 = f32[4,256,1,256]{3,2,1,0:T(1,128)S(1)} fusion(f32[4,3,256,1]{1,3,2,0:T(1,128)S(1)} %copy.67, f32[4,3,256,256]{3,2,1,0:T(8,128)} %get-tuple-element.189), kind=kOutput, calls=%fused_computation.10.clone.1 | convolution fusion | flops 9437184 | bytes 4206592 | tf_op jit(solution)/shard_map/while/body/eval_jaxpr/kcij,kci->kij/dot_general | solution.py:35
  244.8 9.7 %fusion.91 = f32[4,256,1,3]{3,2,1,0:T(1,128)S(1)} fusion(f32[4,3,256,256]{3,2,1,0:T(8,128)S(1)} %copy-done.1, f32[4,256,256,1]{2,1,0,3:T(8,128)S(1)} %fusion.90), kind=kOutput, calls=%fused_computation.12.clone.1 | convolution fusion | flops 9437184 | bytes 4206592 | tf_op jit(solution)/shard_map/while/body/eval_jaxpr/kcij,kij->kci/dot_general | solution.py:36
  260.9 11.7 %fusion.86 = f32[4,256,1,256]{3,2,1,0:T(1,128)S(1)} fusion(f32[4,3,256,1]{1,3,2,0:T(1,128)S(1)} %copy.67, f32[4,3,256,256]{3,2,1,0:T(8,128)} %get-tuple-element.189), kind=kOutput, calls=%fused_computation.10.clone.1 | convolution fusion | flops 9437184 | bytes 4206592 | tf_op jit(solution)/shard_map/while/body/eval_jaxpr/kcij,kci->kij/dot_general | solution.py:35
  278.0 9.7 %fusion.91 = f32[4,256,1,3]{3,2,1,0:T(1,128)S(1)} fusion(f32[4,3,256,256]{3,2,1,0:T(8,128)S(1)} %copy-done.1, f32[4,256,256,1]{2,1,0,3:T(8,128)S(1)} %fusion.90), kind=kOutput, calls=%fused_computation.12.clone.1 | convolution fusion | flops 9437184 | bytes 4206592 | tf_op jit(solution)/shard_map/while/body/eval_jaxpr/kcij,kij->kci/dot_general | solution.py:36
  294.1 11.7 %fusion.86 = f32[4,256,1,256]{3,2,1,0:T(1,128)S(1)} fusion(f32[4,3,256,1]{1,3,2,0:T(1,128)S(1)} %copy.67, f32[4,3,256,256]{3,2,1,0:T(8,128)} %get-tuple-element.189), kind=kOutput, calls=%fused_computation.10.clone.1 | convolution fusion | flops 9437184 | bytes 4206592 | tf_op jit(solution)/shard_map/while/body/eval_jaxpr/kcij,kci->kij/dot_general | solution.py:35
  327.3 11.7 %fusion.86 = f32[4,256,1,256]{3,2,1,0:T(1,128)S(1)} fusion(f32[4,3,256,1]{1,3,2,0:T(1,128)S(1)} %copy.67, f32[4,3,256,256]{3,2,1,0:T(8,128)} %get-tuple-element.189), kind=kOutput, calls=%fused_computation.10.clone.1 | convolution fusion | flops 9437184 | bytes 4206592 | tf_op jit(solution)/shard_map/while/body/eval_jaxpr/kcij,kci->kij/dot_general | solution.py:35
  344.4 9.7 %fusion.91 = f32[4,256,1,3]{3,2,1,0:T(1,128)S(1)} fusion(f32[4,3,256,256]{3,2,1,0:T(8,128)S(1)} %copy-done.1, f32[4,256,256,1]{2,1,0,3:T(8,128)S(1)} %fusion.90), kind=kOutput, calls=%fused_computation.12.clone.1 | convolution fusion | flops 9437184 | bytes 4206592 | tf_op jit(solution)/shard_map/while/body/eval_jaxpr/kcij,kij->kci/dot_general | solution.py:36
  360.5 11.7 %fusion.86 = f32[4,256,1,256]{3,2,1,0:T(1,128)S(1)} fusion(f32[4,3,256,1]{1,3,2,0:T(1,128)S(1)} %copy.67, f32[4,3,256,256]{3,2,1,0:T(8,128)} %get-tuple-element.189), kind=kOutput, calls=%fused_computation.10.clone.1 | convolution fusion | flops 9437184 | bytes 4206592 | tf_op jit(solution)/shard_map/while/body/eval_jaxpr/kcij,kci->kij/dot_general | solution.py:35
  377.6 9.7 %fusion.91 = f32[4,256,1,3]{3,2,1,0:T(1,128)S(1)} fusion(f32[4,3,256,256]{3,2,1,0:T(8,128)S(1)} %copy-done.1, f32[4,256,256,1]{2,1,0,3:T(8,128)S(1)} %fusion.90), kind=kOutput, calls=%fused_computation.12.clone.1 | convolution fusion | flops 9437184 | bytes 4206592 | tf_op jit(solution)/shard_map/while/body/eval_jaxpr/kcij,kij->kci/dot_general | solution.py:36
  393.6 11.6 %fusion.86 = f32[4,256,1,256]{3,2,1,0:T(1,128)S(1)} fusion(f32[4,3,256,1]{1,3,2,0:T(1,128)S(1)} %copy.67, f32[4,3,256,256]{3,2,1,0:T(8,128)} %get-tuple-element.189), kind=kOutput, calls=%fused_computation.10.clone.1 | convolution fusion | flops 9437184 | bytes 4206592 | tf_op jit(solution)/shard_map/while/body/eval_jaxpr/kcij,kci->kij/dot_general | solution.py:35
  426.8 11.7 %fusion.86 = f32[4,256,1,256]{3,2,1,0:T(1,128)S(1)} fusion(f32[4,3,256,1]{1,3,2,0:T(1,128)S(1)} %copy.67, f32[4,3,256,256]{3,2,1,0:T(8,128)} %get-tuple-element.189), kind=kOutput, calls=%fused_computation.10.clone.1 | convolution fusion | flops 9437184 | bytes 4206592 | tf_op jit(solution)/shard_map/while/body/eval_jaxpr/kcij,kci->kij/dot_general | solution.py:35
  460.0 11.7 %fusion.86 = f32[4,256,1,256]{3,2,1,0:T(1,128)S(1)} fusion(f32[4,3,256,1]{1,3,2,0:T(1,128)S(1)} %copy.67, f32[4,3,256,256]{3,2,1,0:T(8,128)} %get-tuple-element.189), kind=kOutput, calls=%fused_computation.10.clone.1 | convolution fusion | flops 9437184 | bytes 4206592 | tf_op jit(solution)/shard_map/while/body/eval_jaxpr/kcij,kci->kij/dot_general | solution.py:35
  493.2 11.7 %fusion.86 = f32[4,256,1,256]{3,2,1,0:T(1,128)S(1)} fusion(f32[4,3,256,1]{1,3,2,0:T(1,128)S(1)} %copy.67, f32[4,3,256,256]{3,2,1,0:T(8,128)} %get-tuple-element.189), kind=kOutput, calls=%fused_computation.10.clone.1 | convolution fusion | flops 9437184 | bytes 4206592 | tf_op jit(solution)/shard_map/while/body/eval_jaxpr/kcij,kci->kij/dot_general | solution.py:35
  510.3 9.7 %fusion.91 = f32[4,256,1,3]{3,2,1,0:T(1,128)S(1)} fusion(f32[4,3,256,256]{3,2,1,0:T(8,128)S(1)} %copy-done.1, f32[4,256,256,1]{2,1,0,3:T(8,128)S(1)} %fusion.90), kind=kOutput, calls=%fused_computation.12.clone.1 | convolution fusion | flops 9437184 | bytes 4206592 | tf_op jit(solution)/shard_map/while/body/eval_jaxpr/kcij,kij->kci/dot_general | solution.py:36
  528.7 72.5 %all-reduce.6.cloned.1.call-done = f32[32,3,256]{2,1,0:T(4,128)} async-done(((f32[32,3,256]{2,1,0:T(4,128)}), f32[32,3,256]{2,1,0:T(4,128)}) %all-reduce.6.cloned.1.call-update) | async-done | bytes 98320
  (360 shorter events, 260.2 us)
Async XLA Ops:
  6.5 47.4 %copy-start = (s32[448,2]{0,1:T(2,128)S(1)}, s32[448,2]{0,1:T(2,128)}, u32[]{:S(2)}) copy-start(s32[448,2]{0,1:T(2,128)} %param.10) | copy-start | bytes 10756
  6.5 594.7 %all-reduce.6.cloned.1.call-start = ((), (), s32[]{:S(2)}) async-start(), calls=%async_computation | async-start | bytes 262144
  47.7 10.0 %collective-permute-start = (f32[32,6,256]{2,1,0:T(8,128)S(1)}, f32[32,6,256]{2,1,0:T(8,128)S(1)}, u32[]{:S(2)}, u32[]{:S(2)}) collective-permute-start(f32[32,6,256]{2,1,0:T(8,128)S(1)} %all_gather.3), channel_id=1, source_target_pairs={{8,0},{16,8},{24,16},{9,1},{17,9},{25,17},{10,2},{18,10},{26,18},{... | collective-permute-start | bytes 589832 | tf_op jit(solution)/shard_map/ppermute | solution.py:19
  57.8 469.6 %copy-start.2 = (u32[32]{0:T(128)S(1)}, u32[32]{0:T(128)}, u32[]{:S(2)}) copy-start(u32[32]{0:T(128)} %constant.277) | copy-start | bytes 388
  77.0 1.9 copy-start.1
  110.2 1.9 copy-start.1
  143.4 1.9 copy-start.1
  176.6 1.9 copy-start.1
  209.8 1.9 copy-start.1
  242.9 1.9 copy-start.1
  276.1 1.9 copy-start.1
  309.3 1.9 copy-start.1
  342.5 1.9 copy-start.1
  375.7 1.9 copy-start.1
  408.9 1.9 copy-start.1
  442.1 1.9 copy-start.1
  475.2 1.9 copy-start.1
  508.4 1.9 copy-start.1
  522.7 4.1 collective-permute-start.1
Sparse Core Ops, SparseCore 0:
  527.6 73.5 all-reduce.5
where the time goes:
time: 614 us; the launch traced here: 613 us
  matrix products  321 us (52%)
  other arithmetic  121 us (20%)
  waiting for transfers between devices  73.5 us (12%)
  local copies, waits for them, and re-layouts  44 us (7%)
  blocking collectives  32.5 us (5%)
  between operations  14.2 us (2%)
    dot_general x14, matrix products, tile_terms(): project_a = jnp.einsum('kcij,kci->kij', offset, loads_a, precision=highest)  163 us
    dot_general x14, matrix products, tile_terms(): jnp.einsum('kcij,kij->kci', offset, dyadic * project_b, precision=highest)  136 us
    unnamed x2, waiting for transfers between devices  72.5 us
    while x14, other arithmetic  40.6 us
    all_gather x1, blocking collectives, body(): slab = lax.all_gather(payload, 'wa', axis=0, tiled=True)  32.5 us
    reduce_sum x14, other arithmetic, tile_terms(): squared = jnp.sum(offset * offset, axis=1) + radius * radius  30.9 us
    dot_general x14, matrix products, tile_terms(): jnp.einsum('kij,kcj->kci', isotropic, loads_b, precision=highest)  13.7 us
  transfers between devices with their start and end apart: 3, of which 2 were waited for; matrix products, arithmetic and copies ran while one was open for 2% of the time, Pallas kernels for 0%

commit v1 on v0

v1 whole, which is shorter than its diff:
```python
import functools
import math

import jax
import jax.numpy as jnp
from jax import lax
from jax.experimental import pallas as pl
from jax.experimental.pallas import tpu as pltpu
from jax.sharding import PartitionSpec as P

BS = 256
ROWS = 8
CHUNK = 32

radius = 0.25
prefactor = 1.0 / (4.0 * math.pi)
half_gauss = 0.5 / math.sqrt(math.pi)
MESH = pl.DeviceIdType.MESH
F32 = jnp.float32
BF16 = jnp.bfloat16

ERFC = (0.565205955, 1.09670851, 2.38765618, -0.0810194158, 14.3292365, -25.4472659, 12.7559653)


def split2(value):
    high = value.astype(BF16)
    return high, (value - high.astype(F32)).astype(BF16)


def split3(value):
    high = value.astype(BF16)
    rest = value - high.astype(F32)
    mid = rest.astype(BF16)
    return high, mid, (rest - mid.astype(F32)).astype(BF16)


def dot(a, b, ca, cb):
    return lax.dot_general(a, b, (((ca,), (cb,)), ((), ())), preferred_element_type=F32)


def pick_kernel(pos_ref, force_ref, order_ref, out_ref):
    per_dev = pos_ref.shape[1]
    pad = jnp.zeros((2, per_dev), F32)
    parts = jnp.concatenate([pos_ref[...], force_ref[...], pad], axis=0)
    parts = jnp.concatenate([p.astype(F32) for p in split3(parts)], axis=0).astype(BF16)
    source = lax.broadcasted_iota(jnp.int32, (per_dev, BS), 0)
    for block in range(per_dev // BS):
        wanted = order_ref[:, block * BS : (block + 1) * BS]
        hot = jnp.where(source == wanted, 1.0, 0.0).astype(BF16)
        got = dot(parts, hot, 1, 0)
        out_ref[block] = (got[0:ROWS] + got[ROWS : 2 * ROWS]) + got[2 * ROWS : 3 * ROWS]


def put_kernel(value_ref, order_ref, out_ref):
    per_dev = out_ref.shape[1]
    nblocks = per_dev // BS
    source = lax.broadcasted_iota(jnp.int32, (per_dev, BS), 0)
    total = None
    for block in range(nblocks):
        value = value_ref[block * ROWS : (block + 1) * ROWS]
        parts = jnp.concatenate([p.astype(F32) for p in split3(value)], axis=0).astype(BF16)
        wanted = order_ref[:, block * BS : (block + 1) * BS]
        hot = jnp.where(source == wanted, 1.0, 0.0).astype(BF16)
        got = dot(parts, hot, 1, 1)
        total = got if total is None else total + got
    total = (total[0:ROWS] + total[ROWS : 2 * ROWS]) + total[2 * ROWS : 3 * ROWS]
    out_ref[...] = total[:3]


def spread_kernel(ngz, nwa, nblocks, mine_ref, out_ref, local_sem, send_sem, recv_sem):
    gz, wa = lax.axis_index("gz"), lax.axis_index("wa")
    lower, upper = gz > 0, gz < ngz - 1
    barrier = pltpu.get_barrier_semaphore()
    for k in range(1, nwa):
        pl.semaphore_signal(barrier, inc=1, device_id=(gz, lax.rem(wa + k, nwa)), device_id_type=MESH)

    @pl.when(upper)
    def _():
        for k in range(nwa):
            pl.semaphore_signal(barrier, inc=1, device_id=(gz + 1, lax.rem(wa + k, nwa)), device_id_type=MESH)

    own = pltpu.make_async_copy(mine_ref, out_ref.at[pl.ds(wa * nblocks, nblocks)], local_sem)
    own.start()
    pl.semaphore_wait(barrier, nwa - 1 + jnp.where(lower, nwa, 0))

    def copy(slot, to_gz, k, base):
        return pltpu.make_async_remote_copy(
            src_ref=mine_ref,
            dst_ref=out_ref.at[pl.ds(slot * nblocks, nblocks)],
            send_sem=send_sem.at[base + k],
            recv_sem=recv_sem.at[slot],
            device_id=(to_gz, lax.rem(wa + k, nwa)),
            device_id_type=MESH,
        )

    @pl.when(lower)
    def _():
        for k in range(nwa):
            copy(nwa + wa, gz - 1, k, nwa).start()

    for k in range(1, nwa):
        copy(wa, gz, k, 0).start()
    own.wait()
    for k in range(1, nwa):
        copy(lax.rem(wa + k, nwa), gz, k, 0).wait_recv()

    @pl.when(upper)
    def _():
        for k in range(nwa):
            copy(nwa + k, gz + 1, k, nwa).wait_recv()

    @pl.when(jnp.logical_not(upper))
    def _():
        out_ref[nwa * nblocks :] = jnp.zeros((nwa * nblocks, ROWS, BS), F32)

    for k in range(1, nwa):
        copy(wa, gz, k, 0).wait_send()

    @pl.when(lower)
    def _():
        for k in range(nwa):
            copy(nwa + wa, gz - 1, k, nwa).wait_send()


def collect_kernel(ngz, nwa, part_ref, out_ref, slots, send_sem, recv_sem):
    gz, wa = lax.axis_index("gz"), lax.axis_index("wa")
    lower, upper = gz > 0, gz < ngz - 1
    barrier = pltpu.get_barrier_semaphore()
    for k in range(1, nwa):
        pl.semaphore_signal(barrier, inc=1, device_id=(gz, lax.rem(wa + k, nwa)), device_id_type=MESH)

    @pl.when(lower)
    def _():
        for k in range(nwa):
            pl.semaphore_signal(barrier, inc=1, device_id=(gz - 1, lax.rem(wa + k, nwa)), device_id_type=MESH)

    pl.semaphore_wait(barrier, nwa - 1 + jnp.where(upper, nwa, 0))

    def copy(slot, to_gz, k, base):
        to = lax.rem(wa + k, nwa)
        return pltpu.make_async_remote_copy(
            src_ref=part_ref.at[base + to],
            dst_ref=slots.at[slot],
            send_sem=send_sem.at[base + k],
            recv_sem=recv_sem.at[slot],
            device_id=(to_gz, to),
            device_id_type=MESH,
        )

    @pl.when(upper)
    def _():
        for k in range(nwa):
            copy(nwa + wa, gz + 1, k, nwa).start()

    for k in range(1, nwa):
        copy(wa, gz, k, 0).start()

    total = part_ref[wa]
    for k in range(1, nwa):
        slot = lax.rem(wa + k, nwa)
        copy(slot, gz, k, 0).wait_recv()
        total = total + slots[slot]
    out_ref[...] = total

    @pl.when(lower)
    def _():
        more = None
        for k in range(nwa):
            copy(nwa + k, gz - 1, k, nwa).wait_recv()
            more = slots[nwa + k] if more is None else more + slots[nwa + k]
        out_ref[...] += more

    for k in range(1, nwa):
        copy(wa, gz, k, 0).wait_send()

    @pl.when(upper)
    def _():
        for k in range(nwa):
            copy(nwa + wa, gz + 1, k, nwa).wait_send()


def pair_values(squared):
    inverse = lax.rsqrt(squared)
    inverse = inverse * (1.5 - (0.5 * squared) * (inverse * inverse))
    distance = squared * inverse
    inverse2 = inverse * inverse
    t = 1.0 / (distance + 2.0)
    series = ERFC[6] * t + ERFC[5]
    for coeff in ERFC[4::-1]:
        series = series * t + coeff
    gauss = jnp.exp(-squared)
    screen = series * t * inverse
    near = inverse2 * (0.5 * radius * radius)
    iso = gauss * (screen * (0.75 + near) + half_gauss)
    dya = (gauss * inverse2) * (screen * (0.75 - 3.0 * near) + half_gauss)
    return iso, dya


def pairs_kernel(nall, nblocks, codes_ref, blocks_ref, out_ref, left, right, feats, acc, tiles, queue):
    rows_codes = codes_ref.shape[0]

    def push(step, count):
        for k in range(8):
            code = codes_ref[step * 8 + k]
            queue[count] = code
            count = count + jnp.where(code >= 0, 1, 0)
        return count

    count = lax.fori_loop(0, rows_codes // 8, push, jnp.int32(0))

    one = jnp.ones((1, BS), F32)
    zero = jnp.zeros((1, BS), F32)

    def prepare(block, carry):
        data = blocks_ref[block]
        x, f = data[0:3], data[3:6]
        high, mid, low = [p.astype(F32) for p in split3(x)]
        norm = jnp.sum(x * x, axis=0, keepdims=True)
        na = [p.astype(F32) for p in split3(norm + radius * radius)]
        nb = [p.astype(F32) for p in split3(norm)]
        left[block] = jnp.concatenate(
            [high, high, mid, high, low, mid, *na, one, one, one, *([zero] * 8)], axis=0
        ).astype(BF16)
        right[block] = jnp.concatenate(
            [-2.0 * p for p in (high, mid, high, low, high, mid)] + [one, one, one, *nb, *([zero] * 8)],
            axis=0,
        ).astype(BF16)
        along = jnp.sum(x * f, axis=0, keepdims=True)
        feat = jnp.concatenate(
            [f, along, f[0:1] * x, f[1:2] * x, f[2:3] * x, along * x], axis=0
        )
        fh, fl = split2(feat)
        feats[block] = jnp.concatenate([fh, fl], axis=0)
        acc[block] = jnp.zeros((24, BS), F32)
        return carry

    lax.fori_loop(0, nall, prepare, 0)

    def gather(block, weight, result_f, result_h):
        acc[block, 0:16] += weight * (result_h[0:16] + result_h[16:32])
        acc[block, 16:24] += weight * (result_f[0:8] + result_f[16:24])

    def pair(step, carry):
        code = queue[step]
        first, second = code // 4096, lax.rem(code, 4096)
        la, rb = left[first], right[second]
        for c in range(BS // CHUNK):
            rows = slice(c * CHUNK, (c + 1) * CHUNK)
            iso, dya = pair_values(dot(la[:, rows], rb, 0, 0))
            fh, fl = split2(iso)
            hh, hl = split2(dya)
            tiles[0, rows] = fh
            tiles[1, rows] = fl
            tiles[2, rows] = hh
            tiles[3, rows] = hl
        fa, fb = feats[first], feats[second]
        gather(
            first,
            1.0,
            dot(fb, tiles[0], 1, 1) + dot(fb, tiles[1], 1, 1),
            dot(fb, tiles[2], 1, 1) + dot(fb, tiles[3], 1, 1),
        )
        gather(
            second,
            jnp.where(first == second, 0.0, 1.0).astype(F32),
            dot(fa, tiles[0], 1, 0) + dot(fa, tiles[1], 1, 0),
            dot(fa, tiles[2], 1, 0) + dot(fa, tiles[3], 1, 0),
        )
        return carry

    lax.fori_loop(0, count, pair, 0)

    def finish(dev, carry):
        for k in range(nblocks):
            block = dev * nblocks + k
            x = blocks_ref[block, 0:3]
            a = acc[block]
            first = jnp.sum(x * a[0:3], axis=0, keepdims=True)
            second = x[0:1] * a[4:7] + x[1:2] * a[7:10] + x[2:3] * a[10:13]
            value = prefactor * (a[16:19] + (x * (first - a[3:4]) - (second - a[13:16])))
            out_ref[dev, k * ROWS : (k + 1) * ROWS] = jnp.concatenate(
                [value, jnp.zeros((ROWS - 3, BS), F32)], axis=0
            )
        return carry

    lax.fori_loop(0, nall // nblocks, finish, 0)


VMEM = pl.BlockSpec(memory_space=pltpu.VMEM)
SMEM = pl.BlockSpec(memory_space=pltpu.SMEM)
LIMIT = 48 * 1024 * 1024


def body(ngz, nwa, positions, forces, order, pair_list, pair_worker):
    per_dev = positions.shape[1]
    nblocks = per_dev // BS
    nall = 2 * nwa * nblocks
    listed = pair_worker.shape[0]
    order = order.reshape(1, per_dev)
    plain = pltpu.CompilerParams(vmem_limit_bytes=LIMIT)
    mine = pl.pallas_call(
        pick_kernel,
        out_shape=jax.ShapeDtypeStruct((nblocks, ROWS, BS), F32),
        in_specs=[VMEM] * 3,
        out_specs=VMEM,
        compiler_params=plain,
    )(positions, forces, order)
    blocks = pl.pallas_call(
        functools.partial(spread_kernel, ngz, nwa, nblocks),
        out_shape=jax.ShapeDtypeStruct((nall, ROWS, BS), F32),
        in_specs=[VMEM],
        out_specs=VMEM,
        scratch_shapes=[
            pltpu.SemaphoreType.DMA,
            pltpu.SemaphoreType.DMA((2 * nwa,)),
            pltpu.SemaphoreType.DMA((2 * nwa,)),
        ],
        compiler_params=pltpu.CompilerParams(
            collective_id=0, has_side_effects=True, vmem_limit_bytes=LIMIT
        ),
    )(mine)
    codes = jnp.where(
        pair_worker == lax.axis_index("wa"), pair_list[:, 0] * 4096 + pair_list[:, 1], -1
    )
    parts = pl.pallas_call(
        functools.partial(pairs_kernel, nall, nblocks),
        out_shape=jax.ShapeDtypeStruct((2 * nwa, nblocks * ROWS, BS), F32),
        in_specs=[SMEM, VMEM],
        out_specs=VMEM,
        scratch_shapes=[
            pltpu.VMEM((nall, 32, BS), BF16),
            pltpu.VMEM((nall, 32, BS), BF16),
            pltpu.VMEM((nall, 32, BS), BF16),
            pltpu.VMEM((nall, 24, BS), F32),
            pltpu.VMEM((4, BS, BS), BF16),
            pltpu.SMEM((listed + 8,), jnp.int32),
        ],
        compiler_params=plain,
    )(codes, blocks)
    owned = pl.pallas_call(
        functools.partial(collect_kernel, ngz, nwa),
        out_shape=jax.ShapeDtypeStruct((nblocks * ROWS, BS), F32),
        in_specs=[VMEM],
        out_specs=VMEM,
        scratch_shapes=[
            pltpu.VMEM((2 * nwa, nblocks * ROWS, BS), F32),
            pltpu.SemaphoreType.DMA((2 * nwa,)),
            pltpu.SemaphoreType.DMA((2 * nwa,)),
        ],
        compiler_params=pltpu.CompilerParams(
            collective_id=1, has_side_effects=True, vmem_limit_bytes=LIMIT
        ),
    )(parts)
    return pl.pallas_call(
        put_kernel,
        out_shape=jax.ShapeDtypeStruct((3, per_dev), F32),
        in_specs=[VMEM] * 2,
        out_specs=VMEM,
        compiler_params=plain,
    )(owned, order)


def solution(mesh):
    return jax.shard_map(
        functools.partial(body, mesh.shape["gz"], mesh.shape["wa"]),
        mesh=mesh,
        in_specs=(
            P(None, ("gz", "wa")),
            P(None, ("gz", "wa")),
            P(("gz", "wa")),
            P("gz", None),
            P("gz"),
        ),
        out_specs=P(None, ("gz", "wa")),
        check_vma=False,
    )
```

time: 614 us -> 80.1 us (0.13)
  matrix products: 321 us -> 0 us
  other arithmetic: 121 us -> 1.46 us
  Pallas kernels: 0 us -> 77.6 us
  waiting for transfers between devices: 73.5 us -> 0 us
  local copies, waits for them, and re-layouts: 44 us -> 0.72 us
  blocking collectives: 32.5 us -> 0 us
  between operations: 14.2 us -> 0.03 us
    dot_general x56 -> x0, matrix products: 321 us -> none  [the longest x14 163 us: tile_terms(): project_a = jnp.einsum('kcij,kci->kij', offset, loads_a, precision=highest)]
    pallas_call x0 -> x5, Pallas kernels: none -> 77.6 us  [the longest x1 50.1 us: body(): pl.pallas_call(functools.partial(pairs_kernel, nall, nblocks), out_shape=...]
    unnamed x2 -> x0, waiting for transfers between devices: 72.5 us -> none
    while x14 -> x0, other arithmetic: 40.6 us -> none
    all_gather x1 -> x0, blocking collectives: 32.5 us -> none  [body(): slab = lax.all_gather(payload, 'wa', axis=0, tiled=True)]
    reduce_sum x15 -> x0, other arithmetic: 32.3 us -> none  [the longest x14 30.9 us: tile_terms(): squared = jnp.sum(offset * offset, axis=1) + radius * radius]
    gather x32 -> x0, local copies, waits for them, and re-layouts: 23.2 us -> none  [the longest x14 7.71 us: step(): block_b = blocks[second_ids]]
    scatter-add x28 -> x0, other arithmetic: 18.4 us -> none  [the longest x14 9.29 us: step(): total = total.at[first_ids].add(weight_a[:, None, None] * result_a)]
  transfers between devices with their start and end apart: 3 -> 0, of which waited for: 2 -> 0; matrix products, arithmetic and copies ran while one was open for 2% -> 0% of each run, Pallas kernels for 0% -> 0%
where the time goes in v1:
time: 80.1 us; the launch traced here: 79.8 us
  Pallas kernels  77.6 us (97%)
  other arithmetic  1.46 us (2%)
    pallas_call x1, Pallas kernels, body(): pl.pallas_call(functools.partial(pairs_kernel, nall, nblocks), out_shape=...  50.1 us
    pallas_call x1, Pallas kernels, body(): pl.pallas_call(functools.partial(collect_kernel, ngz, nwa), out_shape=jax...  14 us
    pallas_call x1, Pallas kernels, body(): pl.pallas_call(functools.partial(spread_kernel, ngz, nwa, nblocks), out_s...  11.7 us

profile of v1, /device:TPU:0, one launch (start us, length us, event | category | flops | bytes accessed | tf_op | source)
XLA Modules:
  0.0 79.8 jit_solution(9672956624294842572)
XLA Ops:
  0.0 0.0 copy-start
  0.0 0.8 slice_add_fusion
  0.8 0.0 copy-start.2
  0.8 0.7 compare_select_fusion.codes_ref
  1.5 0.0 copy-done
  1.5 0.0 copy-done.2
  1.5 0.0 copy-start.1
  1.5 0.7 copy-done.1
  2.2 0.5 shard_map.55.mine_ref
  2.7 11.7 %shard_map.56.blocks_ref = f32[64,8,256]{2,1,0:T(8,128)S(1)} custom-call(f32[4,8,256]{2,1,0:T(8,128)S(1)} %shard_map.55.mine_ref), custom_call_target="tpu_custom_call" | custom-call | tf_op jit(solution)/shard_map/pallas_call | solution.py:308
  14.4 50.1 %shard_map.57.part_ref = f32[16,32,256]{2,1,0:T(8,128)S(1)} custom-call(s32[448]{0:T(512)S(1)} %compare_select_fusion.codes_ref, f32[64,8,256]{2,1,0:T(8,128)S(1)} %shard_map.56.blocks_ref), custom_call_target="tpu_custom_call" | custom-call | tf_op jit(solution)/shard_map/pallas_call | solution.py:325
  64.5 14.0 %shard_map.58.value_ref = f32[32,256]{1,0:T(8,128)S(1)} custom-call(f32[16,32,256]{2,1,0:T(8,128)S(1)} %shard_map.57.part_ref), custom_call_target="tpu_custom_call" | custom-call | tf_op jit(solution)/shard_map/pallas_call | solution.py:340
  78.4 1.3 %shard_map.59 = f32[3,1024]{1,0:T(4,128)} custom-call(f32[32,256]{1,0:T(8,128)S(1)} %shard_map.58.value_ref, s32[1,1024]{1,0:T(1,128)S(1)} %bitcast.3), custom_call_target="tpu_custom_call" | custom-call | tf_op jit(solution)/shard_map/pallas_call | solution.py:354
Async XLA Ops:
  0.0 1.5 %copy-start = (f32[3,1024]{1,0:T(4,128)S(1)}, f32[3,1024]{1,0:T(4,128)}, u32[]{:S(2)}) copy-start(f32[3,1024]{1,0:T(4,128)} %pos_ref.1) | copy-start | bytes 36868
  0.8 0.7 copy-start.2
  1.5 0.7 copy-start.1

commit v2 on v1

--- a/solution.py
+++ b/solution.py
@@ -10,7 +10,9 @@
 
 BS = 256
 ROWS = 8
-CHUNK = 32
+SENT = 6
+BACK = 16
+CHUNK = 64
 
 radius = 0.25
 prefactor = 1.0 / (4.0 * math.pi)
@@ -48,7 +50,8 @@
         wanted = order_ref[:, block * BS : (block + 1) * BS]
         hot = jnp.where(source == wanted, 1.0, 0.0).astype(BF16)
         got = dot(parts, hot, 1, 0)
-        out_ref[block] = (got[0:ROWS] + got[ROWS : 2 * ROWS]) + got[2 * ROWS : 3 * ROWS]
+        got = (got[0:ROWS] + got[ROWS : 2 * ROWS]) + got[2 * ROWS : 3 * ROWS]
+        out_ref[block * SENT : (block + 1) * SENT] = got[0:SENT]
 
 
 def put_kernel(value_ref, order_ref, out_ref):
@@ -57,7 +60,9 @@
     source = lax.broadcasted_iota(jnp.int32, (per_dev, BS), 0)
     total = None
     for block in range(nblocks):
-        value = value_ref[block * ROWS : (block + 1) * ROWS]
+        value = jnp.concatenate(
+            [value_ref[3 * block : 3 * block + 3], jnp.zeros((ROWS - 3, BS), F32)], axis=0
+        )
         parts = jnp.concatenate([p.astype(F32) for p in split3(value)], axis=0).astype(BF16)
         wanted = order_ref[:, block * BS : (block + 1) * BS]
         hot = jnp.where(source == wanted, 1.0, 0.0).astype(BF16)
@@ -67,7 +72,7 @@
     out_ref[...] = total[:3]
 
 
-def spread_kernel(ngz, nwa, nblocks, mine_ref, out_ref, local_sem, send_sem, recv_sem):
+def spread_kernel(ngz, nwa, mine_ref, out_ref, local_sem, send_sem, recv_sem):
     gz, wa = lax.axis_index("gz"), lax.axis_index("wa")
     lower, upper = gz > 0, gz < ngz - 1
     barrier = pltpu.get_barrier_semaphore()
@@ -76,50 +81,64 @@
 
     @pl.when(upper)
     def _():
-        for k in range(nwa):
-            pl.semaphore_signal(barrier, inc=1, device_id=(gz + 1, lax.rem(wa + k, nwa)), device_id_type=MESH)
-
-    own = pltpu.make_async_copy(mine_ref, out_ref.at[pl.ds(wa * nblocks, nblocks)], local_sem)
+        pl.semaphore_signal(barrier, inc=1, device_id=(gz + 1, wa), device_id_type=MESH)
+
+    own = pltpu.make_async_copy(mine_ref, out_ref.at[wa], local_sem)
     own.start()
-    pl.semaphore_wait(barrier, nwa - 1 + jnp.where(lower, nwa, 0))
-
-    def copy(slot, to_gz, k, base):
+    pl.semaphore_wait(barrier, nwa - 1 + jnp.where(lower, 1, 0))
+
+    def across(slot, k):
         return pltpu.make_async_remote_copy(
             src_ref=mine_ref,
-            dst_ref=out_ref.at[pl.ds(slot * nblocks, nblocks)],
-            send_sem=send_sem.at[base + k],
+            dst_ref=out_ref.at[slot],
+            send_sem=send_sem.at[k],
             recv_sem=recv_sem.at[slot],
-            device_id=(to_gz, lax.rem(wa + k, nwa)),
+            device_id=(gz, lax.rem(wa + k, nwa)),
             device_id_type=MESH,
         )
 
+    def down(k, to_gz):
+        slot = lax.rem(wa + k, nwa)
+        return pltpu.make_async_remote_copy(
+            src_ref=mine_ref if k == 0 else out_ref.at[slot],
+            dst_ref=out_ref.at[nwa + slot],
+            send_sem=send_sem.at[nwa + k],
+            recv_sem=recv_sem.at[nwa + slot],
+            device_id=(to_gz, wa),
+            device_id_type=MESH,
+        )
+
+    for k in range(1, nwa):
+        across(wa, k).start()
+
     @pl.when(lower)
     def _():
-        for k in range(nwa):
-            copy(nwa + wa, gz - 1, k, nwa).start()
-
-    for k in range(1, nwa):
-        copy(wa, gz, k, 0).start()
+        down(0, gz - 1).start()
+
     own.wait()
     for k in range(1, nwa):
-        copy(lax.rem(wa + k, nwa), gz, k, 0).wait_recv()
+        across(lax.rem(wa + k, nwa), k).wait_recv()
+
+        @pl.when(lower)
+        def _():
+            down(k, gz - 1).start()
 
     @pl.when(upper)
     def _():
         for k in range(nwa):
-            copy(nwa + k, gz + 1, k, nwa).wait_recv()
+            down(k, gz + 1).wait_recv()
 
     @pl.when(jnp.logical_not(upper))
     def _():
-        out_ref[nwa * nblocks :] = jnp.zeros((nwa * nblocks, ROWS, BS), F32)
-
-    for k in range(1, nwa):
-        copy(wa, gz, k, 0).wait_send()
+        out_ref[nwa:] = jnp.zeros((nwa,) + mine_ref.shape, F32)
+
+    for k in range(1, nwa):
+        across(wa, k).wait_send()
 
     @pl.when(lower)
     def _():
         for k in range(nwa):
-            copy(nwa + wa, gz - 1, k, nwa).wait_send()
+            down(k, gz - 1).wait_send()
 
 
 def collect_kernel(ngz, nwa, part_ref, out_ref, slots, send_sem, recv_sem):
@@ -181,22 +200,24 @@
 
 def pair_values(squared):
     inverse = lax.rsqrt(squared)
-    inverse = inverse * (1.5 - (0.5 * squared) * (inverse * inverse))
     distance = squared * inverse
     inverse2 = inverse * inverse
-    t = 1.0 / (distance + 2.0)
+    shifted = distance + 2.0
+    t = pl.reciprocal(shifted, approx=True)
+    t = t * (2.0 - shifted * t)
     series = ERFC[6] * t + ERFC[5]
     for coeff in ERFC[4::-1]:
         series = series * t + coeff
-    gauss = jnp.exp(-squared)
-    screen = series * t * inverse
-    near = inverse2 * (0.5 * radius * radius)
-    iso = gauss * (screen * (0.75 + near) + half_gauss)
-    dya = (gauss * inverse2) * (screen * (0.75 - 3.0 * near) + half_gauss)
+    gauss = jnp.exp2(squared * (-1.0 / math.log(2.0)))
+    screen = series * (t * inverse)
+    near = (screen * inverse2) * (0.5 * radius * radius)
+    far = 0.75 * screen + half_gauss
+    iso = gauss * (far + near)
+    dya = (gauss * inverse2) * (far - 3.0 * near)
     return iso, dya
 
 
-def pairs_kernel(nall, nblocks, codes_ref, blocks_ref, out_ref, left, right, feats, acc, tiles, queue):
+def pairs_kernel(nall, nblocks, codes_ref, blocks_ref, out_ref, left, right, feats, acc, tiles, tiles_b, queue):
     rows_codes = codes_ref.shape[0]
 
     def push(step, count):
@@ -211,9 +232,13 @@
     one = jnp.ones((1, BS), F32)
     zero = jnp.zeros((1, BS), F32)
 
-    def prepare(block, carry):
-        data = blocks_ref[block]
-        x, f = data[0:3], data[3:6]
+    def prepare_all(dev, carry):
+        for k in range(nblocks):
+            data = blocks_ref[dev, k * SENT : (k + 1) * SENT]
+            prepare(dev * nblocks + k, data[0:3], data[3:6])
+        return carry
+
+    def prepare(block, x, f):
         high, mid, low = [p.astype(F32) for p in split3(x)]
         norm = jnp.sum(x * x, axis=0, keepdims=True)
         na = [p.astype(F32) for p in split3(norm + radius * radius)]
@@ -232,55 +257,69 @@
         fh, fl = split2(feat)
         feats[block] = jnp.concatenate([fh, fl], axis=0)
         acc[block] = jnp.zeros((24, BS), F32)
-        return carry
-
-    lax.fori_loop(0, nall, prepare, 0)
+
+    lax.fori_loop(0, nall // nblocks, prepare_all, 0)
 
     def gather(block, weight, result_f, result_h):
         acc[block, 0:16] += weight * (result_h[0:16] + result_h[16:32])
         acc[block, 16:24] += weight * (result_f[0:8] + result_f[16:24])
 
-    def pair(step, carry):
+    def evaluate(step, into):
         code = queue[step]
-        first, second = code // 4096, lax.rem(code, 4096)
-        la, rb = left[first], right[second]
+        la, rb = left[code // 4096], right[lax.rem(code, 4096)]
         for c in range(BS // CHUNK):
             rows = slice(c * CHUNK, (c + 1) * CHUNK)
             iso, dya = pair_values(dot(la[:, rows], rb, 0, 0))
             fh, fl = split2(iso)
             hh, hl = split2(dya)
-            tiles[0, rows] = fh
-            tiles[1, rows] = fl
-            tiles[2, rows] = hh
-            tiles[3, rows] = hl
+            into[0, rows] = fh
+            into[1, rows] = fl
+            into[2, rows] = hh
+            into[3, rows] = hl
+
+    def apply(step, held):
+        live = jnp.logical_and(step >= 0, step < count)
+        code = queue[jnp.maximum(step, 0)]
+        first, second = code // 4096, lax.rem(code, 4096)
         fa, fb = feats[first], feats[second]
+        both = jnp.logical_and(live, first != second)
         gather(
             first,
-            1.0,
-            dot(fb, tiles[0], 1, 1) + dot(fb, tiles[1], 1, 1),
-            dot(fb, tiles[2], 1, 1) + dot(fb, tiles[3], 1, 1),
+            jnp.where(live, 1.0, 0.0).astype(F32),
+            dot(fb, held[0], 1, 1) + dot(fb, held[1], 1, 1),
+            dot(fb, held[2], 1, 1) + dot(fb, held[3], 1, 1),
         )
         gather(
             second,
-            jnp.where(first == second, 0.0, 1.0).astype(F32),
-            dot(fa, tiles[0], 1, 0) + dot(fa, tiles[1], 1, 0),
-            dot(fa, tiles[2], 1, 0) + dot(fa, tiles[3], 1, 0),
-        )
+            jnp.where(both, 1.0, 0.0).astype(F32),
+            dot(fa, held[0], 1, 0) + dot(fa, held[1], 1, 0),
+            dot(fa, held[2], 1, 0) + dot(fa, held[3], 1, 0),
+        )
+
+    queue[count] = 0
+    tiles_b[...] = jnp.zeros((4, BS, BS), BF16)
+
+    def two(step, carry):
+        evaluate(2 * step, tiles)
+        apply(2 * step - 1, tiles_b)
+        evaluate(2 * step + 1, tiles_b)
+        apply(2 * step, tiles)
         return carry
 
-    lax.fori_loop(0, count, pair, 0)
+    steps = (count + 1) // 2
+    lax.fori_loop(0, steps, two, 0)
+    apply(2 * steps - 1, tiles_b)
 
     def finish(dev, carry):
+        values = []
         for k in range(nblocks):
-            block = dev * nblocks + k
-            x = blocks_ref[block, 0:3]
-            a = acc[block]
+            x = blocks_ref[dev, k * SENT : k * SENT + 3]
+            a = acc[dev * nblocks + k]
             first = jnp.sum(x * a[0:3], axis=0, keepdims=True)
             second = x[0:1] * a[4:7] + x[1:2] * a[7:10] + x[2:3] * a[10:13]
-            value = prefactor * (a[16:19] + (x * (first - a[3:4]) - (second - a[13:16])))
-            out_ref[dev, k * ROWS : (k + 1) * ROWS] = jnp.concatenate(
-                [value, jnp.zeros((ROWS - 3, BS), F32)], axis=0
-            )
+            values.append(prefactor * (a[16:19] + (x * (first - a[3:4]) - (second - a[13:16]))))
+        values.append(jnp.zeros((BACK - 3 * nblocks, BS), F32))
+        out_ref[dev] = jnp.concatenate(values, axis=0)
         return carry
 
     lax.fori_loop(0, nall // nblocks, finish, 0)
@@ -300,14 +339,14 @@
     plain = pltpu.CompilerParams(vmem_limit_bytes=LIMIT)
     mine = pl.pallas_call(
         pick_kernel,
-        out_shape=jax.ShapeDtypeStruct((nblocks, ROWS, BS), F32),
+        out_shape=jax.ShapeDtypeStruct((nblocks * SENT, BS), F32),
         in_specs=[VMEM] * 3,
         out_specs=VMEM,
         compiler_params=plain,
     )(positions, forces, order)
     blocks = pl.pallas_call(
-        functools.partial(spread_kernel, ngz, nwa, nblocks),
-        out_shape=jax.ShapeDtypeStruct((nall, ROWS, BS), F32),
+        functools.partial(spread_kernel, ngz, nwa),
+        out_shape=jax.ShapeDtypeStruct((2 * nwa, nblocks * SENT, BS), F32),
         in_specs=[VMEM],
         out_specs=VMEM,
         scratch_shapes=[
@@ -324,7 +363,7 @@
     )
     parts = pl.pallas_call(
         functools.partial(pairs_kernel, nall, nblocks),
-        out_shape=jax.ShapeDtypeStruct((2 * nwa, nblocks * ROWS, BS), F32),
+        out_shape=jax.ShapeDtypeStruct((2 * nwa, BACK, BS), F32),
         in_specs=[SMEM, VMEM],
         out_specs=VMEM,
         scratch_shapes=[
@@ -333,17 +372,18 @@
             pltpu.VMEM((nall, 32, BS), BF16),
             pltpu.VMEM((nall, 24, BS), F32),
             pltpu.VMEM((4, BS, BS), BF16),
+            pltpu.VMEM((4, BS, BS), BF16),
             pltpu.SMEM((listed + 8,), jnp.int32),
         ],
         compiler_params=plain,
     )(codes, blocks)
     owned = pl.pallas_call(
         functools.partial(collect_kernel, ngz, nwa),
-        out_shape=jax.ShapeDtypeStruct((nblocks * ROWS, BS), F32),
+        out_shape=jax.ShapeDtypeStruct((BACK, BS), F32),
         in_specs=[VMEM],
         out_specs=VMEM,
         scratch_shapes=[
-            pltpu.VMEM((2 * nwa, nblocks * ROWS, BS), F32),
+            pltpu.VMEM((2 * nwa, BACK, BS), F32),
             pltpu.SemaphoreType.DMA((2 * nwa,)),
             pltpu.SemaphoreType.DMA((2 * nwa,)),
         ],

time: 80.1 us -> 56.3 us (0.70)
  Pallas kernels: 77.6 us -> 53.7 us
    pallas_call x1, Pallas kernels: 50.1 us -> 32.5 us  [body(): pl.pallas_call(functools.partial(pairs_kernel, nall, nblocks), out_shape=...]
    pallas_call x1, Pallas kernels: 14 us -> 8.86 us  [body(): pl.pallas_call(functools.partial(collect_kernel, ngz, nwa), out_shape=jax...]
    pallas_call x2, Pallas kernels: 12.2 us -> 11 us  [the longest x1 10.5 us: body(): pl.pallas_call(functools.partial(spread_kernel, ngz, nwa), out_shape=jax....]
where the time goes in v2:
time: 56.3 us; the launch traced here: 56 us
  Pallas kernels  53.7 us (95%)
  other arithmetic  1.46 us (3%)
  local copies, waits for them, and re-layouts  0.72 us (1%)
    pallas_call x1, Pallas kernels, body(): pl.pallas_call(functools.partial(pairs_kernel, nall, nblocks), out_shape=...  32.5 us
    pallas_call x1, Pallas kernels, body(): pl.pallas_call(functools.partial(spread_kernel, ngz, nwa), out_shape=jax....  10.5 us
    pallas_call x1, Pallas kernels, body(): pl.pallas_call(functools.partial(collect_kernel, ngz, nwa), out_shape=jax...  8.86 us
    pallas_call x1, Pallas kernels, body(): pl.pallas_call(put_kernel, out_shape=jax.ShapeDtypeStruct((3, per_dev), F...  1.34 us

profile of v2, /device:TPU:0, one launch (start us, length us, event | category | flops | bytes accessed | tf_op | source)
XLA Modules:
  0.0 56.0 jit_solution(662201084417796461)
XLA Ops:
  0.0 0.0 copy-start
  0.0 0.8 %slice_add_fusion = s32[448,1]{0,1:T(1,128)S(1)} fusion(s32[448,2]{0,1:T(2,128)} %param.8), kind=kLoop, calls=%fused_computation | loop fusion | flops 896 | bytes 5376 | tf_op jit(solution)/shard_map/add | solution.py:362
  0.8 0.0 copy-start.2
  0.8 0.7 %compare_select_fusion.codes_ref = s32[448]{0:T(512)S(1)} fusion(s32[448]{0:T(512)S(1)} %bitcast.4, s32[448]{0:T(512)} %param.9, s32[]{:T(128)S(6)} %axis_index.12), kind=kLoop, calls=%fused_computation.1 | loop fusion | flops 896 | bytes 5380 | tf_op jit(solution)/shard_map/jit(_where)/select_n | solution.py:361
  1.5 0.0 copy-done
  1.5 0.0 copy-done.2
  1.5 0.0 copy-start.1
  1.5 0.7 %copy-done.1 = f32[3,1024]{1,0:T(4,128)S(1)} copy-done((f32[3,1024]{1,0:T(4,128)S(1)}, f32[3,1024]{1,0:T(4,128)}, u32[]{:S(2)}) %copy-start.1) | copy-done | bytes 12312
  2.2 0.5 shard_map.55.mine_ref
  2.7 10.5 %shard_map.56.blocks_ref = f32[16,24,256]{2,1,0:T(8,128)S(1)} custom-call(f32[24,256]{1,0:T(8,128)S(1)} %shard_map.55.mine_ref), custom_call_target="tpu_custom_call" | custom-call | tf_op jit(solution)/shard_map/pallas_call | solution.py:347
  13.2 32.5 %shard_map.57.part_ref = f32[16,16,256]{2,1,0:T(8,128)S(1)} custom-call(s32[448]{0:T(512)S(1)} %compare_select_fusion.codes_ref, f32[16,24,256]{2,1,0:T(8,128)S(1)} %shard_map.56.blocks_ref), custom_call_target="tpu_custom_call" | custom-call | tf_op jit(solution)/shard_map/pallas_call | solution.py:364
  45.7 8.9 %shard_map.58.value_ref = f32[16,256]{1,0:T(8,128)S(1)} custom-call(f32[16,16,256]{2,1,0:T(8,128)S(1)} %shard_map.57.part_ref), custom_call_target="tpu_custom_call" | custom-call | tf_op jit(solution)/shard_map/pallas_call | solution.py:380
  54.6 1.3 %shard_map.59 = f32[3,1024]{1,0:T(4,128)} custom-call(f32[16,256]{1,0:T(8,128)S(1)} %shard_map.58.value_ref, s32[1,1024]{1,0:T(1,128)S(1)} %bitcast.3), custom_call_target="tpu_custom_call" | custom-call | tf_op jit(solution)/shard_map/pallas_call | solution.py:394
Async XLA Ops:
  0.0 1.5 %copy-start = (f32[3,1024]{1,0:T(4,128)S(1)}, f32[3,1024]{1,0:T(4,128)}, u32[]{:S(2)}) copy-start(f32[3,1024]{1,0:T(4,128)} %pos_ref.1) | copy-start | bytes 36868
  0.8 0.7 %copy-start.2 = (s32[1024]{0:T(1024)S(1)}, s32[1024]{0:T(1024)}, u32[]{:S(2)}) copy-start(s32[1024]{0:T(1024)} %param.7) | copy-start | bytes 12292
  1.5 0.7 %copy-start.1 = (f32[3,1024]{1,0:T(4,128)S(1)}, f32[3,1024]{1,0:T(4,128)}, u32[]{:S(2)}) copy-start(f32[3,1024]{1,0:T(4,128)} %force_ref.1) | copy-start | bytes 36868

commit v3 on v2

--- a/solution.py
+++ b/solution.py
@@ -40,7 +40,17 @@
     return lax.dot_general(a, b, (((ca,), (cb,)), ((), ())), preferred_element_type=F32)
 
 
-def pick_kernel(pos_ref, force_ref, order_ref, out_ref):
+def pick_kernel(*refs):
+    sources, (out_ref, codes_ref), held, sems = refs[:5], refs[5:7], refs[7:12], refs[12]
+    copies = [pltpu.make_async_copy(a, b, sems.at[k]) for k, (a, b) in enumerate(zip(sources, held))]
+    for copy in copies:
+        copy.start()
+    for copy in copies:
+        copy.wait()
+    pos_ref, force_ref, order_ref, list_ref, worker_ref = held
+    codes_ref[...] = jnp.where(
+        worker_ref[...] == lax.axis_index("wa"), list_ref[0:1] * 4096 + list_ref[1:2], -1
+    )
     per_dev = pos_ref.shape[1]
     pad = jnp.zeros((2, per_dev), F32)
     parts = jnp.concatenate([pos_ref[...], force_ref[...], pad], axis=0)
@@ -218,11 +228,11 @@
 
 
 def pairs_kernel(nall, nblocks, codes_ref, blocks_ref, out_ref, left, right, feats, acc, tiles, tiles_b, queue):
-    rows_codes = codes_ref.shape[0]
+    rows_codes = codes_ref.shape[1]
 
     def push(step, count):
         for k in range(8):
-            code = codes_ref[step * 8 + k]
+            code = codes_ref[0, step * 8 + k]
             queue[count] = code
             count = count + jnp.where(code >= 0, 1, 0)
         return count
@@ -337,13 +347,24 @@
     listed = pair_worker.shape[0]
     order = order.reshape(1, per_dev)
     plain = pltpu.CompilerParams(vmem_limit_bytes=LIMIT)
-    mine = pl.pallas_call(
+    mine, codes = pl.pallas_call(
         pick_kernel,
-        out_shape=jax.ShapeDtypeStruct((nblocks * SENT, BS), F32),
-        in_specs=[VMEM] * 3,
-        out_specs=VMEM,
+        out_shape=(
+            jax.ShapeDtypeStruct((nblocks * SENT, BS), F32),
+            jax.ShapeDtypeStruct((1, listed), jnp.int32),
+        ),
+        in_specs=[pl.BlockSpec(memory_space=pl.ANY)] * 5,
+        out_specs=(VMEM, VMEM),
+        scratch_shapes=[
+            pltpu.VMEM((3, per_dev), F32),
+            pltpu.VMEM((3, per_dev), F32),
+            pltpu.VMEM((1, per_dev), jnp.int32),
+            pltpu.VMEM((2, listed), jnp.int32),
+            pltpu.VMEM((1, listed), jnp.int32),
+            pltpu.SemaphoreType.DMA((5,)),
+        ],
         compiler_params=plain,
-    )(positions, forces, order)
+    )(positions, forces, order, pair_list.T, pair_worker.reshape(1, listed))
     blocks = pl.pallas_call(
         functools.partial(spread_kernel, ngz, nwa),
         out_shape=jax.ShapeDtypeStruct((2 * nwa, nblocks * SENT, BS), F32),
@@ -358,9 +379,6 @@
             collective_id=0, has_side_effects=True, vmem_limit_bytes=LIMIT
         ),
     )(mine)
-    codes = jnp.where(
-        pair_worker == lax.axis_index("wa"), pair_list[:, 0] * 4096 + pair_list[:, 1], -1
-    )
     parts = pl.pallas_call(
         functools.partial(pairs_kernel, nall, nblocks),
         out_shape=jax.ShapeDtypeStruct((2 * nwa, BACK, BS), F32),

time: 56.3 us -> 57.7 us (1.025)
  local copies, waits for them, and re-layouts: 0.72 us -> 3.49 us
  other arithmetic: 1.46 us -> 0 us
    unnamed x6 -> x10, local copies, waits for them, and re-layouts: 0.72 us -> 3.49 us
    add x1 -> x0, other arithmetic: 0.77 us -> none  [body(): pair_list[:, 0] * 4096 + pair_list[:, 1]]
    select_n x1 -> x0, other arithmetic: 0.7 us -> none  [body(): jnp.where(pair_worker == lax.axis_index('wa'), pair_list[:, 0] * 4096 + p...]
where the time goes in v3:
time: 57.7 us; the launch traced here: 57.4 us
  Pallas kernels  53.8 us (93%)
  local copies, waits for them, and re-layouts  3.49 us (6%)
    pallas_call x1, Pallas kernels, body(): pl.pallas_call(functools.partial(pairs_kernel, nall, nblocks), out_shape=...  32.5 us
    pallas_call x1, Pallas kernels, body(): pl.pallas_call(functools.partial(spread_kernel, ngz, nwa), out_shape=jax....  10.6 us
    pallas_call x1, Pallas kernels, body(): pl.pallas_call(functools.partial(collect_kernel, ngz, nwa), out_shape=jax...  8.85 us
    unnamed x10, local copies, waits for them, and re-layouts  3.49 us
    pallas_call x1, Pallas kernels, body(): pl.pallas_call(put_kernel, out_shape=jax.ShapeDtypeStruct((3, per_dev), F...  1.34 us

profile of v3, /device:TPU:0, one launch (start us, length us, event | category | flops | bytes accessed | tf_op | source)
XLA Modules:
  0.0 57.4 jit_solution(6421631186436358966)
XLA Ops:
  0.0 0.0 copy-start.2
  0.0 0.7 %copy-done.2 = s32[1024]{0:T(1024)S(1)} copy-done((s32[1024]{0:T(1024)S(1)}, s32[1024]{0:T(1024)}, u32[]{:S(2)}) %copy-start.2) | copy-done | bytes 4120
  0.7 0.0 copy-start
  0.7 0.7 %copy-done = f32[3,1024]{1,0:T(4,128)S(1)} copy-done((f32[3,1024]{1,0:T(4,128)S(1)}, f32[3,1024]{1,0:T(4,128)}, u32[]{:S(2)}) %copy-start) | copy-done | bytes 12312
  1.4 0.0 copy-start.1
  1.4 0.7 %copy-done.1 = f32[3,1024]{1,0:T(4,128)S(1)} copy-done((f32[3,1024]{1,0:T(4,128)S(1)}, f32[3,1024]{1,0:T(4,128)}, u32[]{:S(2)}) %copy-start.1) | copy-done | bytes 12312
  2.1 0.0 copy-start.3
  2.1 0.7 %copy-done.3 = s32[448,2]{0,1:T(2,128)S(1)} copy-done((s32[448,2]{0,1:T(2,128)S(1)}, s32[448,2]{0,1:T(2,128)}, u32[]{:S(2)}) %copy-start.3) | copy-done | bytes 3608
  2.8 0.0 copy-start.4
  2.8 0.7 %copy-done.4 = s32[448]{0:T(512)S(1)} copy-done((s32[448]{0:T(512)S(1)}, s32[448]{0:T(512)}, u32[]{:S(2)}) %copy-start.4) | copy-done | bytes 1816
  3.5 0.5 shard_map.55
  4.0 10.6 %shard_map.56.blocks_ref = f32[16,24,256]{2,1,0:T(8,128)S(1)} custom-call(f32[24,256]{1,0:T(8,128)S(1)} %get-tuple-element.8.mine_ref), custom_call_target="tpu_custom_call" | custom-call | tf_op jit(solution)/shard_map/pallas_call | solution.py:368
  14.6 32.5 %shard_map.57.part_ref = f32[16,16,256]{2,1,0:T(8,128)S(1)} custom-call(s32[1,448]{1,0:T(1,128)S(1)} %get-tuple-element.7.codes_ref, f32[16,24,256]{2,1,0:T(8,128)S(1)} %shard_map.56.blocks_ref), custom_call_target="tpu_custom_call" | custom-call | tf_op jit(solution)/shard_map/pallas_call | solution.py:382
  47.1 8.9 %shard_map.58.value_ref = f32[16,256]{1,0:T(8,128)S(1)} custom-call(f32[16,16,256]{2,1,0:T(8,128)S(1)} %shard_map.57.part_ref), custom_call_target="tpu_custom_call" | custom-call | tf_op jit(solution)/shard_map/pallas_call | solution.py:398
  56.0 1.3 %shard_map.59 = f32[3,1024]{1,0:T(4,128)} custom-call(f32[16,256]{1,0:T(8,128)S(1)} %shard_map.58.value_ref, s32[1,1024]{1,0:T(1,128)S(1)} %bitcast.4), custom_call_target="tpu_custom_call" | custom-call | tf_op jit(solution)/shard_map/pallas_call | solution.py:412
Async XLA Ops:
  0.0 0.7 %copy-start.2 = (s32[1024]{0:T(1024)S(1)}, s32[1024]{0:T(1024)}, u32[]{:S(2)}) copy-start(s32[1024]{0:T(1024)} %param.7) | copy-start | bytes 12292
  0.7 0.7 %copy-start = (f32[3,1024]{1,0:T(4,128)S(1)}, f32[3,1024]{1,0:T(4,128)}, u32[]{:S(2)}) copy-start(f32[3,1024]{1,0:T(4,128)} %refs_0_.1) | copy-start | bytes 36868
  1.4 0.7 %copy-start.1 = (f32[3,1024]{1,0:T(4,128)S(1)}, f32[3,1024]{1,0:T(4,128)}, u32[]{:S(2)}) copy-start(f32[3,1024]{1,0:T(4,128)} %refs_1_.1) | copy-start | bytes 36868
  2.1 0.7 %copy-start.3 = (s32[448,2]{0,1:T(2,128)S(1)}, s32[448,2]{0,1:T(2,128)}, u32[]{:S(2)}) copy-start(s32[448,2]{0,1:T(2,128)} %param.8) | copy-start | bytes 10756
  2.8 0.7 %copy-start.4 = (s32[448]{0:T(512)S(1)}, s32[448]{0:T(512)}, u32[]{:S(2)}) copy-start(s32[448]{0:T(512)} %param.9) | copy-start | bytes 5380
